TPU v7x, 32 devices: a whole 2x2x4 slice. The times are simulated.
32 devices in a mesh: wide: 16 (over z, y, x), grp: 2 (over core).
Axes of the slice: x: 2, y: 2, z: 4, core: 2. Of those that a mesh axis runs over, the one named last changes fastest.
Arguments:
- samples: bfloat16 [128, 512], P(('wide', 'grp')), may hold values from -6 to 6
- archive: bfloat16 [16384, 512], P(('wide', 'grp')), may hold values from -6 to 6
- inv_len: float32 [512], replicated, may hold values from 0.7 to 2.8
- mean_coef: bfloat16 [16384, 64], P(('wide', 'grp')), may hold values from -0.75 to 0.75
- var_coef: bfloat16 [16384, 64], P(('wide', 'grp')), may hold values from -4 to 4
Outputs:
- pred_mean: float32 [128, 64], P(('wide', 'grp'))
- pred_var: float32 [128, 64], P(('wide', 'grp'))
All inputs are finite; a program needn't handle non-finite values.
Results may differ from a plain program's by a relative error of at most 0.0085.
Values may be sent and summed in bfloat16 or wider, within the bound.
No kernel may reach another device: no remote copies, remote signals or barrier semaphores. Data moves between devices by JAX's collectives and lax.ppermute only.
A program may use at most 64 MiB of HBM per device.

v0:
```python
import jax
import jax.numpy as jnp
from jax import lax
from jax.experimental import pallas as pl
from jax.experimental.pallas import tpu as pltpu
from jax.sharding import PartitionSpec as P

DIN = 512
AXES = ("wide", "grp")
RANKS = ("grp", "wide")
PAIR = 2
BLOCK = 128
NORM_ROWS = 16
VMEM_LIMIT = 40 * 1024 * 1024


def scaled(rows, inv_len):
    factor = inv_len * DIN ** (-0.5)
    return (rows.astype(jnp.float32) * factor).astype(jnp.bfloat16)


def send_kernel(
    samples_hbm, inv_len_hbm, archive_hbm, mean_hbm, var_hbm,
    sent_ref, inv_len_ref, archive_ref, coefs_ref, samples_ref, arrived,
):
    width = mean_hbm.shape[0]
    copies = [
        pltpu.make_async_copy(source, target, arrived.at[number])
        for number, (source, target) in enumerate((
            (archive_hbm, archive_ref),
            (mean_hbm, coefs_ref.at[pl.ds(0, width)]),
            (var_hbm, coefs_ref.at[pl.ds(width, width)]),
            (samples_hbm, samples_ref),
            (inv_len_hbm, inv_len_ref),
        ))
    ]
    for copy in copies:
        copy.start()
    for copy in copies[3:]:
        copy.wait()
    samp_z = scaled(samples_ref[...], inv_len_ref[...])
    samp_z = samp_z.reshape((1, PAIR, 1) + sent_ref.shape[3:])
    sent_ref[...] = jnp.broadcast_to(samp_z, sent_ref.shape)
    for copy in copies[:3]:
        copy.wait()


def runs_kernel(inv_len_ref, archive_ref, coefs_ref, pack_ref):
    runs = archive_ref.shape[0]
    width = coefs_ref.shape[0] // 2
    row = lax.broadcasted_iota(jnp.int32, (BLOCK, BLOCK), 0)
    column = lax.broadcasted_iota(jnp.int32, (BLOCK, BLOCK), 1)
    norms = []
    for first in range(0, runs, BLOCK):
        arch_z = scaled(archive_ref[first : first + BLOCK, :], inv_len_ref[...])
        turned = arch_z.T
        pack_ref[:DIN, first : first + BLOCK] = turned
        products = jnp.dot(arch_z, turned, preferred_element_type=jnp.float32)
        norms.append(jnp.sum(jnp.where(row == column, products, 0.0), axis=0, keepdims=True))
    coefs = coefs_ref[...]
    for first in range(0, runs, 2 * width):
        block = slice(first, first + 2 * width)
        pack_ref[DIN : DIN + 2 * width, block] = coefs[:, block].T
    rest = jnp.broadcast_to(0.5 * jnp.concatenate(norms, axis=1), (NORM_ROWS, runs))
    part_row = lax.broadcasted_iota(jnp.int32, rest.shape, 0)
    parts = jnp.zeros(rest.shape, jnp.float32)
    for number in range(3):
        part = rest.astype(jnp.bfloat16).astype(jnp.float32)
        parts = jnp.where(part_row == number, part, parts)
        rest = rest - part
    pack_ref[DIN + 2 * width :, :] = parts.astype(jnp.bfloat16)


def sums_kernel(slots_ref, own_ref, peer_ref, sums_ref):
    width = sums_ref.shape[1] // 2
    packs = (own_ref, peer_ref)
    slots, part_rows, _ = slots_ref.shape

    def block(first, count):
        samp_z = slots_ref[pl.ds(first, count)].reshape(count * part_rows, DIN)
        wide_copy = samp_z.astype(jnp.float32)
        samp_norm = 0.5 * jnp.sum(wide_copy * wide_copy, axis=-1, keepdims=True)
        arch_z = jnp.concatenate([pack_ref[:DIN, :] for pack_ref in packs], axis=1)
        inner_prod = jnp.dot(samp_z, arch_z, preferred_element_type=jnp.float32)
        norm_parts = jnp.concatenate([pack_ref[DIN + 2 * width :, :] for pack_ref in packs], axis=1)
        arch_norm = jnp.sum(norm_parts.astype(jnp.float32), axis=0, keepdims=True)
        kernel = jnp.exp(inner_prod - samp_norm - arch_norm)
        both = jnp.concatenate([kernel, kernel * kernel], axis=0).astype(jnp.bfloat16)
        coefs = jnp.concatenate(
            [
                pack_ref[DIN : DIN + 2 * width, first : first + 2 * width]
                for pack_ref in packs
                for first in range(0, pack_ref.shape[1], 2 * width)
            ],
            axis=0,
        )
        total = jnp.dot(both, coefs, preferred_element_type=jnp.float32)
        rows = count * part_rows
        lane = lax.broadcasted_iota(jnp.int32, (rows, 2 * width), 1)
        sums = jnp.where(lane < width, total[:rows], total[rows:])
        sums_ref[pl.ds(pl.multiple_of(first * part_rows, rows), rows), :] = sums

    step = min(slots, BLOCK // part_rows)
    if step == slots:
        block(0, slots)
    else:
        @pl.loop(0, slots // step)
        def _(number):
            block(number * step, step)


def outputs_kernel(parts_ref, mean_hbm, var_hbm, mean_ref, var_ref, written):
    width = mean_ref.shape[1]
    summed = jnp.sum(parts_ref[...], axis=(0, 2))
    summed = summed.reshape(mean_ref.shape[0], 2 * width)
    mean_ref[...] = summed[:, :width]
    mean_copy = pltpu.make_async_copy(mean_ref, mean_hbm, written.at[0])
    mean_copy.start()
    var_ref[...] = 1.0 - summed[:, width:]
    var_copy = pltpu.make_async_copy(var_ref, var_hbm, written.at[1])
    var_copy.start()
    mean_copy.wait()
    var_copy.wait()


def call(kernel, out_shape, inputs, flops, transcendentals=0, in_space=pltpu.VMEM, scratch=()):
    moved = sum(array.size * array.dtype.itemsize for array in inputs)
    return pl.pallas_call(
        kernel,
        out_shape=out_shape,
        in_specs=[pl.BlockSpec(memory_space=in_space)] * len(inputs),
        out_specs=jax.tree.map(lambda out: pl.BlockSpec(memory_space=out.memory_space), out_shape),
        scratch_shapes=scratch,
        cost_estimate=pl.CostEstimate(
            flops=flops, bytes_accessed=moved, transcendentals=transcendentals
        ),
        compiler_params=pltpu.CompilerParams(vmem_limit_bytes=VMEM_LIMIT),
    )(*inputs)


def on_device(samples, archive, inv_len, mean_coef, var_coef):
    devices = lax.axis_size(AXES)
    grp = lax.axis_size("grp")
    own_rows = samples.shape[0]
    part_rows = own_rows // PAIR
    rows = devices * part_rows
    slots = (grp // PAIR, PAIR, lax.axis_size("wide"))
    runs, width = mean_coef.shape

    arrays = (samples, inv_len.reshape(1, DIN), archive, mean_coef.T, var_coef.T)
    sent, *held = call(
        send_kernel,
        (pltpu.VMEM(slots + (part_rows, DIN), jnp.bfloat16),)
        + tuple(pltpu.VMEM(array.shape, array.dtype) for array in arrays[1:3])
        + (pltpu.VMEM((2 * width, runs), mean_coef.dtype),),
        [pltpu.with_memory_space_constraint(array, pltpu.HBM) for array in arrays],
        flops=own_rows * DIN,
        in_space=pltpu.HBM,
        scratch=[pltpu.VMEM(samples.shape, samples.dtype), pltpu.SemaphoreType.DMA((5,))],
    )
    gathered = lax.all_to_all(sent.reshape(devices, part_rows, DIN), RANKS, split_axis=0, concat_axis=0, tiled=True)
    own = call(
        runs_kernel,
        pltpu.VMEM((DIN + 2 * width + NORM_ROWS, runs), jnp.bfloat16),
        held,
        flops=2 * BLOCK * runs * DIN,
    )
    peer = lax.ppermute(own, "grp", [(i, i ^ 1) for i in range(grp)])
    sums = call(
        sums_kernel,
        pltpu.VMEM((rows, 2 * width), jnp.float32),
        (gathered, own, peer),
        flops=4 * rows * runs * (DIN + 4 * width),
        transcendentals=2 * rows * runs,
    )
    sums = sums.reshape(devices, part_rows, 2 * width)
    parts = lax.all_to_all(sums, RANKS, split_axis=0, concat_axis=0, tiled=True)
    return tuple(call(
        outputs_kernel,
        (pltpu.HBM((own_rows, width), jnp.float32),) * 2,
        (parts.reshape(slots + (part_rows, 2 * width)),),
        flops=parts.size,
        scratch=[pltpu.VMEM((own_rows, width), jnp.float32)] * 2 + [pltpu.SemaphoreType.DMA((2,))],
    ))


def solution(mesh):
    rows = P(AXES, None)
    return jax.shard_map(
        on_device,
        mesh=mesh,
        in_specs=(rows, rows, P(), rows, rows),
        out_specs=(rows, rows),
        check_vma=False,
    )
```

profile of v0, /device:TPU:0, one launch (start us, length us, event | category | flops | bytes accessed | tf_op | source)
XLA Modules:
  0.0 26.8 jit_solution(7942639883499859859)
XLA Ops:
  0.6 1.1 %shard_map.68 = (bf16[1,2,16,2,512]{4,3,2,1,0:T(2,128)(2,1)S(1)}, f32[1,512]{1,0:T(1,128)S(1)}, bf16[512,512]{1,0:T(8,128)(2,1)S(1)}, bf16[128,512]{1,0:T(8,128)(2,1)S(1)}) custom-call(bf16[4,512]{1,0:T(4,128)(2,1)} %samples_hbm.1, f32[1,512]{1,0:T(1,128)} %bitcast.11, bf16[512,512]{1,0:T(8,128)(2,1)} %archive_hbm.1, bf16[64,512]{1,0:T(8,128)(2,1)} %bitcast.9, ...), custom_call_target="tpu_custom_call" | custom-call | flops 2048 | bytes 661504 | tf_op jit(solution)/shard_map/pallas_call | solution.py:128
  1.7 0.4 %shard_map.69.own_ref = bf16[656,512]{1,0:T(8,128)(2,1)S(1)} custom-call(f32[1,512]{1,0:T(1,128)S(1)} %get-tuple-element.7.inv_len_ref, bf16[512,512]{1,0:T(8,128)(2,1)S(1)} %get-tuple-element.8.archive_ref, bf16[128,512]{1,0:T(8,128)(2,1)S(1)} %get-tuple-element.9.coefs_ref), custom_call_target="tpu_custom_call" | custom-call | flops 67108864 | bytes 657408 | tf_op jit(solution)/shard_map/pallas_call | solution.py:128
  2.1 0.5 %collective-permute-start = (bf16[656,512]{1,0:T(8,128)(2,1)S(1)}, bf16[656,512]{1,0:T(8,128)(2,1)S(1)}, u32[]{:S(2)}, u32[]{:S(2)}) collective-permute-start(bf16[656,512]{1,0:T(8,128)(2,1)S(1)} %shard_map.69.own_ref), channel_id=1, source_target_pairs={{0,1},{1,0},{2,3},{3,2},{4,5},{5,4},{6,7},{7,6},{8,9},{9,8},{10,11... | collective-permute-start | bytes 2015240 | tf_op jit(solution)/shard_map/ppermute | solution.py:168
  2.6 14.1 %all_to_all.10.slots_ref = bf16[32,2,512]{2,1,0:T(2,128)(2,1)S(1)} all-to-all(bf16[32,2,512]{2,1,0:T(2,128)(2,1)S(1)} %bitcast.8), channel_id=1, replica_groups=mesh['wide'=16,'grp'=2] {'grp','wide'}, dimensions={0} | all-to-all | bytes 131072 | tf_op jit(solution)/shard_map/all_to_all | solution.py:161
  16.7 0.0 collective-permute-done.peer_ref
  16.7 0.5 %shard_map.70 = f32[64,128]{1,0:T(8,128)S(1)} custom-call(bf16[32,2,512]{2,1,0:T(2,128)(2,1)S(1)} %all_to_all.10.slots_ref, bf16[656,512]{1,0:T(8,128)(2,1)S(1)} %shard_map.69.own_ref, bf16[656,512]{1,0:T(8,128)(2,1)S(1)} %collective-permute-done.peer_ref), custom_call_target="tpu_custom_call" | custom-call | flops 100663296 | bytes 1409024 | tf_op jit(solution)/shard_map/pallas_call | solution.py:128
  17.2 8.9 %all_to_all.11 = f32[32,2,128]{2,1,0:T(2,128)S(1)} all-to-all(f32[32,2,128]{2,1,0:T(2,128)S(1)} %bitcast.6), channel_id=1, replica_groups=mesh['wide'=16,'grp'=2] {'grp','wide'}, dimensions={0} | all-to-all | bytes 65536 | tf_op jit(solution)/shard_map/all_to_all | solution.py:177
  26.1 0.7 %shard_map.71 = (f32[4,64]{1,0:T(4,128)}, f32[4,64]{1,0:T(4,128)}) custom-call(f32[1,2,16,2,128]{4,3,2,1,0:T(2,128)S(1)} %bitcast.7), custom_call_target="tpu_custom_call" | custom-call | flops 8192 | bytes 32768 | tf_op jit(solution)/shard_map/pallas_call | solution.py:128
Async XLA Ops:
  2.1 14.6 %collective-permute-start = (bf16[656,512]{1,0:T(8,128)(2,1)S(1)}, bf16[656,512]{1,0:T(8,128)(2,1)S(1)}, u32[]{:S(2)}, u32[]{:S(2)}) collective-permute-start(bf16[656,512]{1,0:T(8,128)(2,1)S(1)} %shard_map.69.own_ref), channel_id=1, source_target_pairs={{0,1},{1,0},{2,3},{3,2},{4,5},{5,4},{6,7},{7,6},{8,9},{9,8},{10,11... | collective-permute-start | bytes 2015240 | tf_op jit(solution)/shard_map/ppermute | solution.py:168
where the time goes:
time: 27 us; the launch traced here: 26.8 us
  blocking collectives  23 us (85%)
  Pallas kernels  2.61 us (10%)
  between operations  0.65 us (2%)
  starting transfers between devices  0.52 us (2%)
    all_to_all x1, blocking collectives, on_device(): lax.all_to_all(sent.reshape(devices, part_rows, DIN), RANKS, split_axis=0...  14.1 us
    all_to_all x1, blocking collectives, on_device(): parts = lax.all_to_all(sums, RANKS, split_axis=0, concat_axis=0, tiled=True)  8.9 us
    pallas_call x4, Pallas kernels, call(): pl.pallas_call(kernel, out_shape=out_shape, in_specs=[pl.BlockSpec(memory...  2.61 us
  transfers between devices with their start and end apart: 1, of which 0 were waited for; matrix products, arithmetic and copies ran while one was open for 0% of the time, Pallas kernels for 0%

commit v1 on v0

--- a/solution.py
+++ b/solution.py
@@ -48,6 +48,10 @@
 def runs_kernel(inv_len_ref, archive_ref, coefs_ref, pack_ref):
     runs = archive_ref.shape[0]
     width = coefs_ref.shape[0] // 2
+    coefs = coefs_ref[...]
+    for first in range(0, runs, 2 * width):
+        block = slice(first, first + 2 * width)
+        pack_ref[DIN : DIN + 2 * width, block] = coefs[:, block].T
     row = lax.broadcasted_iota(jnp.int32, (BLOCK, BLOCK), 0)
     column = lax.broadcasted_iota(jnp.int32, (BLOCK, BLOCK), 1)
     norms = []
@@ -57,10 +61,6 @@
         pack_ref[:DIN, first : first + BLOCK] = turned
         products = jnp.dot(arch_z, turned, preferred_element_type=jnp.float32)
         norms.append(jnp.sum(jnp.where(row == column, products, 0.0), axis=0, keepdims=True))
-    coefs = coefs_ref[...]
-    for first in range(0, runs, 2 * width):
-        block = slice(first, first + 2 * width)
-        pack_ref[DIN : DIN + 2 * width, block] = coefs[:, block].T
     rest = jnp.broadcast_to(0.5 * jnp.concatenate(norms, axis=1), (NORM_ROWS, runs))
     part_row = lax.broadcasted_iota(jnp.int32, rest.shape, 0)
     parts = jnp.zeros(rest.shape, jnp.float32)

time: 27 us -> 27 us (level)
  no operation moved by 1% of the time
where the time goes in v1:
time: 27 us; the launch traced here: 26.8 us
  blocking collectives  23 us (85%)
  Pallas kernels  2.61 us (10%)
  between operations  0.65 us (2%)
  starting transfers between devices  0.52 us (2%)
    all_to_all x1, blocking collectives, on_device(): lax.all_to_all(sent.reshape(devices, part_rows, DIN), RANKS, split_axis=0...  14.1 us
    all_to_all x1, blocking collectives, on_device(): parts = lax.all_to_all(sums, RANKS, split_axis=0, concat_axis=0, tiled=True)  8.9 us
    pallas_call x4, Pallas kernels, call(): pl.pallas_call(kernel, out_shape=out_shape, in_specs=[pl.BlockSpec(memory...  2.61 us
  transfers between devices with their start and end apart: 1, of which 0 were waited for; matrix products, arithmetic and copies ran while one was open for 0% of the time, Pallas kernels for 0%

profile of v1, /device:TPU:0, one launch (start us, length us, event | category | flops | bytes accessed | tf_op | source)
XLA Modules:
  0.0 26.8 jit_solution(7942639883499859859)
XLA Ops:
  0.6 1.1 %shard_map.68 = (bf16[1,2,16,2,512]{4,3,2,1,0:T(2,128)(2,1)S(1)}, f32[1,512]{1,0:T(1,128)S(1)}, bf16[512,512]{1,0:T(8,128)(2,1)S(1)}, bf16[128,512]{1,0:T(8,128)(2,1)S(1)}) custom-call(bf16[4,512]{1,0:T(4,128)(2,1)} %samples_hbm.1, f32[1,512]{1,0:T(1,128)} %bitcast.11, bf16[512,512]{1,0:T(8,128)(2,1)} %archive_hbm.1, bf16[64,512]{1,0:T(8,128)(2,1)} %bitcast.9, ...), custom_call_target="tpu_custom_call" | custom-call | flops 2048 | bytes 661504 | tf_op jit(solution)/shard_map/pallas_call | solution.py:128
  1.7 0.4 %shard_map.69.own_ref = bf16[656,512]{1,0:T(8,128)(2,1)S(1)} custom-call(f32[1,512]{1,0:T(1,128)S(1)} %get-tuple-element.7.inv_len_ref, bf16[512,512]{1,0:T(8,128)(2,1)S(1)} %get-tuple-element.8.archive_ref, bf16[128,512]{1,0:T(8,128)(2,1)S(1)} %get-tuple-element.9.coefs_ref), custom_call_target="tpu_custom_call" | custom-call | flops 67108864 | bytes 657408 | tf_op jit(solution)/shard_map/pallas_call | solution.py:128
  2.1 0.5 %collective-permute-start = (bf16[656,512]{1,0:T(8,128)(2,1)S(1)}, bf16[656,512]{1,0:T(8,128)(2,1)S(1)}, u32[]{:S(2)}, u32[]{:S(2)}) collective-permute-start(bf16[656,512]{1,0:T(8,128)(2,1)S(1)} %shard_map.69.own_ref), channel_id=1, source_target_pairs={{0,1},{1,0},{2,3},{3,2},{4,5},{5,4},{6,7},{7,6},{8,9},{9,8},{10,11... | collective-permute-start | bytes 2015240 | tf_op jit(solution)/shard_map/ppermute | solution.py:168
  2.6 14.1 %all_to_all.10.slots_ref = bf16[32,2,512]{2,1,0:T(2,128)(2,1)S(1)} all-to-all(bf16[32,2,512]{2,1,0:T(2,128)(2,1)S(1)} %bitcast.8), channel_id=1, replica_groups=mesh['wide'=16,'grp'=2] {'grp','wide'}, dimensions={0} | all-to-all | bytes 131072 | tf_op jit(solution)/shard_map/all_to_all | solution.py:161
  16.7 0.0 collective-permute-done.peer_ref
  16.7 0.5 %shard_map.70 = f32[64,128]{1,0:T(8,128)S(1)} custom-call(bf16[32,2,512]{2,1,0:T(2,128)(2,1)S(1)} %all_to_all.10.slots_ref, bf16[656,512]{1,0:T(8,128)(2,1)S(1)} %shard_map.69.own_ref, bf16[656,512]{1,0:T(8,128)(2,1)S(1)} %collective-permute-done.peer_ref), custom_call_target="tpu_custom_call" | custom-call | flops 100663296 | bytes 1409024 | tf_op jit(solution)/shard_map/pallas_call | solution.py:128
  17.2 8.9 %all_to_all.11 = f32[32,2,128]{2,1,0:T(2,128)S(1)} all-to-all(f32[32,2,128]{2,1,0:T(2,128)S(1)} %bitcast.6), channel_id=1, replica_groups=mesh['wide'=16,'grp'=2] {'grp','wide'}, dimensions={0} | all-to-all | bytes 65536 | tf_op jit(solution)/shard_map/all_to_all | solution.py:177
  26.1 0.7 %shard_map.71 = (f32[4,64]{1,0:T(4,128)}, f32[4,64]{1,0:T(4,128)}) custom-call(f32[1,2,16,2,128]{4,3,2,1,0:T(2,128)S(1)} %bitcast.7), custom_call_target="tpu_custom_call" | custom-call | flops 8192 | bytes 32768 | tf_op jit(solution)/shard_map/pallas_call | solution.py:128
Async XLA Ops:
  2.1 14.6 %collective-permute-start = (bf16[656,512]{1,0:T(8,128)(2,1)S(1)}, bf16[656,512]{1,0:T(8,128)(2,1)S(1)}, u32[]{:S(2)}, u32[]{:S(2)}) collective-permute-start(bf16[656,512]{1,0:T(8,128)(2,1)S(1)} %shard_map.69.own_ref), channel_id=1, source_target_pairs={{0,1},{1,0},{2,3},{3,2},{4,5},{5,4},{6,7},{7,6},{8,9},{9,8},{10,11... | collective-permute-start | bytes 2015240 | tf_op jit(solution)/shard_map/ppermute | solution.py:168
